TPU v7x, 32 devices: a whole 2x2x4 slice. The times are simulated.
32 devices in a mesh: wide: 8 (over z, y), tp: 4 (over x, core).
Axes of the slice: x: 2, y: 2, z: 4, core: 2. Of those that a mesh axis runs over, the one named last changes fastest.
Arguments:
- tokens: bfloat16 [16384, 768], P(('wide', 'tp')), may hold values from -6 to 6
- query_weight: bfloat16 [768, 768], P('wide', 'tp'), may hold values from -0.02734375 to 0.02734375
- key_weight: bfloat16 [768, 768], P('wide', 'tp'), may hold values from -0.21875 to 0.21875
- value_weight: bfloat16 [768, 768], P('wide', 'tp'), may hold values from -0.21875 to 0.21875
- out_weight: bfloat16 [768, 768], P('wide', 'tp'), may hold values from -1.25 to 1.25
- attn_gain: bfloat16 [768], P('wide'), may hold values from 0.5 to 1.5
- ff_gain: bfloat16 [768], P('wide'), may hold values from 0.5 to 1.5
- router: bfloat16 [768, 16], P('wide'), may hold values from -0.109375 to 0.109375
- expert_in: bfloat16 [16, 768, 3072], P('wide', None, 'tp'), may hold values from -0.21875 to 0.21875
- expert_out: bfloat16 [16, 3072, 768], P('wide', 'tp')
- bias_table: bfloat16 [12, 32], replicated, may hold values from -4 to 4
- routes: int32 [16384, 1], P(('wide', 'tp')), may hold values from 0 to 15; in each aligned block of 512 rows (0 to 511, 512 to 1023, ...) at most 40 rows name the same one
- keep: int32 [16384], P(('wide', 'tp')), may hold values 0 or 1
- cotangent: bfloat16 [16384, 768], P(('wide', 'tp')), may hold values from -6 to 6
Outputs:
- block_out: float32 [16384, 768], P(('wide', 'tp'))
- input_grad: float32 [16384, 768], P(('wide', 'tp'))
- query_grad: float32 [768, 768], P('wide', 'tp')
- key_grad: float32 [768, 768], P('wide', 'tp')
- value_grad: float32 [768, 768], P('wide', 'tp')
- out_grad: float32 [768, 768], P('wide', 'tp')
- attn_gain_grad: float32 [768], P('wide')
- ff_gain_grad: float32 [768], P('wide')
- router_grad: float32 [768, 16], P('wide')
- expert_in_grad: float32 [16, 768, 3072], P('wide', None, 'tp')
- expert_out_grad: float32 [16, 3072, 768], P('wide', 'tp')
- bias_grad: float32 [12, 32], replicated
Inputs may be any that keep to these rules, and one draw needn't show every extreme that they name: `routes`: in each aligned block of 512 rows (the rows of one device) no expert is named by more than 40 rows, and one is named by exactly 40.
All inputs are finite; a program needn't handle non-finite values. No bound on the sum of `keep` on one device may be relied on, other than what follows from the above.
Results may differ from a plain program's by a relative error of at most 0.02.
Values may be sent and summed in bfloat16 or wider, within the bound.
A program may use at most 192 MiB of HBM per device.

v0:
```python
from functools import partial

import jax
import jax.numpy as jnp
from jax import lax
from jax.experimental import pallas as pl
from jax.experimental.pallas import tpu as pltpu
from jax.sharding import PartitionSpec as P

HEAD = 64
BUCKETS = 32
LEN = 1024


epsilon = 1e-06
highest = lax.Precision.HIGHEST
bucket_bounds = [12, 16, 23, 32, 46, 64, 91]


BLOCK = 256


def bucket_onehot(length, buckets):
    half = buckets // 2
    exact = half // 2
    offset = jnp.arange(-length, length, dtype=jnp.int32)
    distance = jnp.abs(offset)
    bounds = jnp.asarray(bucket_bounds, dtype=jnp.int32)
    far = exact + jnp.sum(
        (distance[:, None] >= bounds[None, :]).astype(jnp.int32), axis=1, dtype=jnp.int32
    )
    far = jnp.minimum(far, half - 1)
    upper = jnp.where(offset > 0, half, 0).astype(jnp.int32)
    table = upper + jnp.where(distance < exact, distance, far)
    return (table[:, None] == jnp.arange(buckets, dtype=jnp.int32)[None, :]).astype(jnp.float32)


def root_norm(value, gain):
    inverse = lax.rsqrt(jnp.mean(value * value, axis=-1, keepdims=True) + epsilon)
    normed = value * inverse
    return (normed, inverse, normed * gain)


def root_norm_back(grad_in, normed, inverse, gain):
    scaled = grad_in * gain
    inner = jnp.mean(scaled * normed, axis=-1, keepdims=True)
    return (inverse * (scaled - normed * inner), jnp.sum(grad_in * normed, axis=0))


def contract_rows(left, right):
    return lax.dot_general(
        left, right, (((0,), (0,)), ((), ())), preferred_element_type=jnp.float32
    )


def contract_cols(left, right):
    return lax.dot_general(
        left, right, (((1,), (1,)), ((), ())), preferred_element_type=jnp.float32
    )


def gather_rows(rows):
    return lax.all_gather(rows, "tp", axis=0, tiled=True)


def sum_rows(term):
    return lax.psum_scatter(
        term.astype(jnp.bfloat16), "tp", scatter_dimension=0, tiled=True
    ).astype(jnp.float32)


def build_bias(heads, rel_ref, bias_ref):
    for h in range(heads):
        row = jnp.broadcast_to(rel_ref[h : h + 1, :], (BLOCK, 2 * LEN))
        bias_ref[h] = pltpu.roll(row, 0, 1, stride=1, stride_axis=0).T


def flip(value):
    return value.astype(jnp.float32).T.astype(jnp.bfloat16)


def stack_heads(parts):
    pad = jnp.zeros((BLOCK - HEAD * len(parts), parts[0].shape[1]), jnp.float32)
    return jnp.concatenate([*parts, pad], axis=0)


def head_lanes(h, value):
    lane = lax.broadcasted_iota(jnp.int32, value.shape, 1)
    return jnp.where((lane >= h * HEAD) & (lane < (h + 1) * HEAD), value, jnp.zeros_like(value))


def forward_kernel(heads, q_ref, k_ref, v_ref, rel_ref, ctx_ref, lse_ref, bias_ref, vt_ref):
    block = pl.program_id(1)

    @pl.when((pl.program_id(0) == 0) & (block == 0))
    def first():
        build_bias(heads, rel_ref, bias_ref)

    @pl.when(block == 0)
    def new_sequence():
        vt_ref[...] = flip(v_ref[...])

    start = pl.multiple_of(LEN - block * BLOCK, BLOCK)
    parts, logs = ([], [])
    for h in range(heads):
        scores = contract_cols(k_ref[...], head_lanes(h, q_ref[...]))
        scores = scores + bias_ref[h, pl.ds(start, LEN), :]
        top = jnp.max(scores, axis=0, keepdims=True)
        expo = jnp.exp(scores - top)
        total = jnp.sum(expo, axis=0, keepdims=True)
        out = jnp.dot(
            vt_ref[h * HEAD : (h + 1) * HEAD, :],
            expo.astype(jnp.bfloat16),
            preferred_element_type=jnp.float32,
        )
        parts.append(out / total)
        logs.append(top + jnp.log(total))
    ctx_ref[...] = stack_heads(parts).T.astype(jnp.bfloat16)
    logs.append(jnp.zeros((8 - heads, BLOCK), jnp.float32))
    lse_ref[0] = jnp.concatenate(logs, axis=0)


def backward_kernel(
    heads,
    q_ref,
    k_ref,
    v_ref,
    g_ref,
    lse_ref,
    rel_ref,
    dq_ref,
    dk_ref,
    dv_ref,
    drel_ref,
    bias_ref,
    kt_ref,
    sum_ref,
    dk_sum,
    dv_sum,
):
    sequence, block = (pl.program_id(0), pl.program_id(1))
    last = pl.num_programs(1) - 1

    @pl.when((sequence == 0) & (block == 0))
    def first():
        build_bias(heads, rel_ref, bias_ref)
        sum_ref[...] = jnp.zeros_like(sum_ref)

    @pl.when(block == 0)
    def new_sequence():
        kt_ref[...] = flip(k_ref[...])
        dk_sum[...] = jnp.zeros_like(dk_sum)
        dv_sum[...] = jnp.zeros_like(dv_sum)

    start = pl.multiple_of(LEN - block * BLOCK, BLOCK)
    parts = []
    for h in range(heads):
        query = head_lanes(h, q_ref[...])
        grad = head_lanes(h, g_ref[...])
        scores = contract_cols(k_ref[...], query) + bias_ref[h, pl.ds(start, LEN), :]
        weights = jnp.exp(scores - lse_ref[0, h : h + 1, :])
        grad_weights = contract_cols(v_ref[...], grad)
        inner = jnp.sum(weights * grad_weights, axis=0, keepdims=True)
        grad_scores = (weights * (grad_weights - inner)).astype(jnp.bfloat16)
        sum_ref[h, pl.ds(start, LEN), :] += grad_scores.astype(jnp.float32)
        parts.append(
            jnp.dot(
                kt_ref[h * HEAD : (h + 1) * HEAD, :],
                grad_scores,
                preferred_element_type=jnp.float32,
            )
        )
        dk_sum[...] += jnp.dot(grad_scores, query, preferred_element_type=jnp.float32)
        dv_sum[...] += jnp.dot(
            weights.astype(jnp.bfloat16), grad, preferred_element_type=jnp.float32
        )
    dq_ref[...] = stack_heads(parts).T.astype(jnp.bfloat16)

    @pl.when(block == last)
    def end_sequence():
        dk_ref[...] = dk_sum[...].astype(jnp.bfloat16)
        dv_ref[...] = dv_sum[...].astype(jnp.bfloat16)

    @pl.when((sequence == pl.num_programs(0) - 1) & (block == last))
    def end_all():
        drel_ref[...] = jnp.zeros_like(drel_ref)
        for h in range(heads):
            rows = sum_ref[h].T
            count = BLOCK
            while count > 1:
                count //= 2
                rows = rows[:count] + pltpu.roll(rows[count:], 2 * LEN - count, 1)
            drel_ref[h : h + 1, :] = rows


def attention_specs(blocks):
    query = pl.BlockSpec((BLOCK, BLOCK), lambda s, b: (s * blocks + b, 0))
    key = pl.BlockSpec((LEN, BLOCK), lambda s, b: (s, 1))
    value = pl.BlockSpec((LEN, BLOCK), lambda s, b: (s, 2))
    whole = pl.BlockSpec((LEN, BLOCK), lambda s, b: (s, 0))
    rel = pl.BlockSpec((8, 2 * LEN), lambda s, b: (0, 0))
    logs = pl.BlockSpec((1, 8, BLOCK), lambda s, b: (s * blocks + b, 0, 0))
    return (query, key, value, whole, rel, logs)


def attend(projected, relative, heads):
    rows = projected.shape[0]
    blocks = LEN // BLOCK
    query, key, value, whole, rel, logs = attention_specs(blocks)
    return pl.pallas_call(
        partial(forward_kernel, heads),
        grid=(rows // LEN, blocks),
        in_specs=[query, key, value, rel],
        out_specs=[query, logs],
        out_shape=[
            jax.ShapeDtypeStruct((rows, BLOCK), jnp.bfloat16),
            jax.ShapeDtypeStruct((rows // BLOCK, 8, BLOCK), jnp.float32),
        ],
        scratch_shapes=[
            pltpu.VMEM((heads, 2 * LEN, BLOCK), jnp.float32),
            pltpu.VMEM((BLOCK, LEN), jnp.bfloat16),
        ],
        compiler_params=pltpu.CompilerParams(vmem_limit_bytes=48 * 2**20),
        name="attend",
    )(projected, projected, projected, relative)


def attend_back(projected, grad_context, logs_in, relative, heads):
    rows = projected.shape[0]
    blocks = LEN // BLOCK
    query, key, value, whole, rel, logs = attention_specs(blocks)
    return pl.pallas_call(
        partial(backward_kernel, heads),
        grid=(rows // LEN, blocks),
        in_specs=[query, key, value, query, logs, rel],
        out_specs=[query, whole, whole, rel],
        out_shape=[
            jax.ShapeDtypeStruct((rows, BLOCK), jnp.bfloat16),
            jax.ShapeDtypeStruct((rows, BLOCK), jnp.bfloat16),
            jax.ShapeDtypeStruct((rows, BLOCK), jnp.bfloat16),
            jax.ShapeDtypeStruct((8, 2 * LEN), jnp.float32),
        ],
        scratch_shapes=[
            pltpu.VMEM((heads, 2 * LEN, BLOCK), jnp.float32),
            pltpu.VMEM((BLOCK, LEN), jnp.bfloat16),
            pltpu.VMEM((heads, 2 * LEN, BLOCK), jnp.float32),
            pltpu.VMEM((LEN, BLOCK), jnp.float32),
            pltpu.VMEM((LEN, BLOCK), jnp.float32),
        ],
        compiler_params=pltpu.CompilerParams(vmem_limit_bytes=48 * 2**20),
        name="attend_back",
    )(projected, projected, projected, grad_context, logs_in, relative)


def per_device(
    tokens,
    query_weight,
    key_weight,
    value_weight,
    out_weight,
    attn_gain,
    ff_gain,
    router,
    expert_in,
    expert_out,
    bias_table,
    routes,
    keep,
    cotangent,
):
    tp_size = lax.axis_size("tp")
    wide_size = lax.axis_size("wide")
    tok_rows, width = tokens.shape
    local_experts = expert_in.shape[0]
    experts = local_experts * wide_size
    capacity = (5 * tok_rows + 4 * experts - 1) // (4 * experts)
    head_width = query_weight.shape[1]
    local_heads = head_width // HEAD
    tokens_all = gather_rows(tokens)
    packed = jnp.concatenate(
        [
            query_weight,
            key_weight,
            value_weight,
            out_weight,
            router,
            attn_gain[:, None],
            ff_gain[:, None],
        ],
        axis=1,
    )
    packed = lax.all_gather(packed, "wide", axis=0, tiled=True)
    side = ((0, 0), (0, BLOCK - head_width))
    w_query, w_key, w_value, w_out = (
        jnp.pad(packed[:, i * head_width : (i + 1) * head_width], side) for i in range(4)
    )
    w_joint = jnp.concatenate([w_query, w_key, w_value], axis=1)
    at = 4 * head_width
    w_router = packed[:, at : at + experts]
    gain_one = packed[:, at + experts].astype(jnp.float32)
    gain_two = packed[:, at + experts + 1].astype(jnp.float32)
    expert_ids = routes[:, 0]
    hot = (expert_ids[:, None] == jnp.arange(experts, dtype=jnp.int32)[None, :]).astype(jnp.float32)
    lower = (jnp.arange(tok_rows)[:, None] > jnp.arange(tok_rows)[None, :]).astype(jnp.bfloat16)
    earlier = jnp.dot(lower, hot.astype(jnp.bfloat16), preferred_element_type=jnp.float32)
    slot = expert_ids * capacity + jnp.sum(earlier * hot, axis=1).astype(jnp.int32)
    dispatch = (jnp.arange(experts * capacity, dtype=jnp.int32)[:, None] == slot[None, :]).astype(
        jnp.bfloat16
    )

    def to_wide(rows):
        placed = jnp.dot(dispatch, rows, preferred_element_type=jnp.float32).astype(jnp.bfloat16)
        placed = placed.reshape(wide_size, local_experts * capacity, width)
        placed = lax.all_to_all(placed, "wide", split_axis=0, concat_axis=0, tiled=True)
        return placed.reshape(experts * capacity, width)

    def by_expert(rows):
        rows = rows.reshape(tp_size, wide_size, local_experts, capacity, width)
        return rows.transpose(2, 0, 1, 3, 4).reshape(local_experts, -1, width)

    def from_owners(terms):
        terms = terms.astype(jnp.bfloat16)
        terms = terms.reshape(local_experts, tp_size, wide_size, capacity, width)
        terms = terms.transpose(1, 2, 0, 3, 4).reshape(-1, width)
        summed = lax.psum_scatter(terms, "tp", scatter_dimension=0, tiled=True)
        summed = summed.reshape(wide_size, local_experts * capacity, width)
        back = lax.all_to_all(summed, "wide", split_axis=0, concat_axis=0, tiled=True)
        return back.reshape(experts * capacity, width)

    kept = cotangent * keep.astype(jnp.bfloat16)[:, None]
    kept_wide = to_wide(kept)
    onehot_table = bucket_onehot(LEN, BUCKETS)
    table_local = lax.dynamic_slice_in_dim(
        bias_table.astype(jnp.float32), lax.axis_index("tp") * local_heads, local_heads, 0
    )
    relative = jnp.pad(
        lax.dot_general(
            table_local, onehot_table, (((1,), (1,)), ((), ())), precision=highest
        ),
        ((0, 8 - local_heads), (0, 0)),
    )
    tokens_all, kept_wide = lax.optimization_barrier((tokens_all, kept_wide))
    kept_all = gather_rows(kept_wide)
    rows_one = root_norm(tokens_all.astype(jnp.float32), gain_one)[2].astype(jnp.bfloat16)
    x_value = tokens.astype(jnp.float32)
    normed_one, inverse_one, scaled_one = root_norm(x_value, gain_one)
    projected = jnp.dot(rows_one, w_joint, preferred_element_type=jnp.float32).astype(jnp.bfloat16)
    context_low, log_totals = attend(projected, relative, local_heads)
    context_low, kept_all = lax.optimization_barrier((context_low, kept_all))
    attended = sum_rows(contract_cols(context_low, w_out))
    hidden = x_value + attended
    normed_two, inverse_two, scaled_two = root_norm(hidden, gain_two)
    rows_two = scaled_two.astype(jnp.bfloat16)
    logits = jnp.dot(rows_two, w_router, preferred_element_type=jnp.float32)
    probs = jax.nn.softmax(logits, axis=-1)
    gate = jnp.sum(probs * hot, axis=-1)
    weight_token = keep.astype(jnp.float32) * gate
    grad_in = cotangent.astype(jnp.float32)
    arrived = by_expert(gather_rows(to_wide(rows_two)))
    kept_slots = by_expert(kept_all)
    kept_act = jnp.einsum(
        "ecd,efd->ecf", kept_slots, expert_out, preferred_element_type=jnp.float32
    )
    own = lax.axis_index("wide") * local_experts + jnp.arange(local_experts, dtype=jnp.int32)
    own_hot = (own[:, None] == jnp.arange(experts, dtype=jnp.int32)[None, :]).astype(jnp.float32)
    slot_logits = jnp.einsum(
        "ecd,dx->ecx", arrived, w_router, preferred_element_type=jnp.float32
    )
    slot_gate = jnp.sum(
        jax.nn.softmax(slot_logits, axis=-1) * own_hot[:, None, :], axis=-1, keepdims=True
    )
    grad_slots = (slot_gate * kept_slots.astype(jnp.float32)).astype(jnp.bfloat16)
    expert_pre = jnp.einsum("ecd,edf->ecf", arrived, expert_in, preferred_element_type=jnp.float32)
    grad_act = slot_gate * kept_act
    act_float, gelu_back = jax.vjp(partial(jax.nn.gelu, approximate=True), expert_pre)
    expert_act = act_float.astype(jnp.bfloat16)
    grad_pre = gelu_back(grad_act)[0].astype(jnp.bfloat16)
    expert_terms = jnp.einsum(
        "ecf,efd->ecd", expert_act, expert_out, preferred_element_type=jnp.float32
    )
    results = from_owners(expert_terms)
    grad_back_terms = jnp.einsum(
        "ecf,edf->ecd", grad_pre, expert_in, preferred_element_type=jnp.float32
    )
    expert_out_grad = jnp.einsum(
        "ecf,ecd->efd", expert_act, grad_slots, preferred_element_type=jnp.float32
    )
    expert_in_grad = jnp.einsum(
        "ecd,ecf->edf", arrived, grad_pre, preferred_element_type=jnp.float32
    )
    returned = contract_rows(dispatch, results)
    grad_input_expert = contract_rows(dispatch, from_owners(grad_back_terms))
    block_out = hidden + weight_token[:, None] * returned
    grad_gate = keep.astype(jnp.float32) * jnp.sum(grad_in * returned, axis=-1)
    grad_logits = ((grad_gate * gate)[:, None] * (hot - probs)).astype(jnp.bfloat16)
    router_full_grad = contract_rows(rows_two, grad_logits)
    grad_normed_two = grad_input_expert + contract_cols(grad_logits, w_router)
    grad_hidden_norm, gain_two_grad = root_norm_back(
        grad_normed_two, normed_two, inverse_two, gain_two
    )
    grad_hidden = grad_in + grad_hidden_norm
    grad_rows = gather_rows(grad_hidden.astype(jnp.bfloat16))
    grad_rows, expert_in_grad, expert_out_grad = lax.optimization_barrier(
        (grad_rows, expert_in_grad, expert_out_grad)
    )
    grad_context = jnp.dot(grad_rows, w_out, preferred_element_type=jnp.float32).astype(
        jnp.bfloat16
    )
    out_full_grad = contract_rows(grad_rows, context_low)
    grad_query, grad_key, grad_value, relative_grad = attend_back(
        projected, grad_context, log_totals, relative, local_heads
    )
    grad_joint = jnp.concatenate([grad_query, grad_key, grad_value], axis=1)
    input_term = contract_cols(grad_joint, w_joint).astype(jnp.bfloat16)
    joint_grad = contract_rows(rows_one, grad_joint)
    gain_one_grad = jnp.sum(joint_grad * w_joint.astype(jnp.float32), axis=1) / gain_one
    bias_local = jnp.dot(relative_grad[:local_heads], onehot_table, precision=highest)
    shard = width // wide_size
    bias_cols = -(-local_heads * BUCKETS // shard)
    bias_flat = jnp.pad(
        bias_local.reshape(-1), (0, bias_cols * shard - local_heads * BUCKETS)
    ).reshape(shard, bias_cols)
    small = jnp.concatenate(
        [
            router_full_grad,
            gain_two_grad[:, None],
            gain_one_grad[:, None],
            jnp.tile(bias_flat, (wide_size, 1)),
        ],
        axis=1,
    )
    high_part = small.astype(jnp.bfloat16)
    low_part = (small - high_part.astype(jnp.float32)).astype(jnp.bfloat16)
    columns = small.shape[1]
    weight_grads = jnp.concatenate(
        [
            joint_grad[:, i * BLOCK : i * BLOCK + head_width].astype(jnp.bfloat16)
            for i in range(3)
        ]
        + [out_full_grad[:, :head_width].astype(jnp.bfloat16), high_part, low_part],
        axis=1,
    )
    weight_grads, input_term = lax.optimization_barrier((weight_grads, input_term))
    weight_grads = lax.all_to_all(
        weight_grads.reshape(wide_size, shard, 4 * head_width + 2 * columns),
        "wide",
        split_axis=0,
        concat_axis=0,
        tiled=True,
    )
    weight_grads = weight_grads.astype(jnp.float32).sum(axis=0)
    query_sum, key_sum, value_sum, out_sum = (
        weight_grads[:, i * head_width : (i + 1) * head_width] for i in range(4)
    )
    at = 4 * head_width
    small = weight_grads[:, at : at + columns] + weight_grads[:, at + columns :]
    grad_normed_one = sum_rows(input_term)
    grad_normed_one, small = lax.optimization_barrier((grad_normed_one, small))
    grad_x_norm, unused = root_norm_back(grad_normed_one, normed_one, inverse_one, gain_one)
    input_grad = grad_hidden + grad_x_norm
    small_all = lax.all_gather(small, "tp", axis=0, tiled=False)
    bias_grad = small_all[:, :, experts + 2 :].reshape(tp_size, -1)
    bias_grad = bias_grad[:, : local_heads * BUCKETS].reshape(bias_table.shape)
    small = small_all.sum(axis=0)
    return (
        block_out,
        input_grad,
        query_sum,
        key_sum,
        value_sum,
        out_sum,
        small[:, experts + 1],
        small[:, experts],
        small[:, :experts],
        expert_in_grad,
        expert_out_grad,
        bias_grad,
    )


def solution(mesh):
    placed = (
        P(("wide", "tp"), None),
        P("wide", "tp"),
        P("wide", "tp"),
        P("wide", "tp"),
        P("wide", "tp"),
        P("wide"),
        P("wide"),
        P("wide", None),
        P("wide", None, "tp"),
        P("wide", "tp", None),
        P(),
        P(("wide", "tp"), None),
        P(("wide", "tp")),
        P(("wide", "tp"), None),
    )
    return jax.shard_map(
        per_device,
        mesh=mesh,
        in_specs=placed,
        out_specs=(
            P(("wide", "tp"), None),
            P(("wide", "tp"), None),
            P("wide", "tp"),
            P("wide", "tp"),
            P("wide", "tp"),
            P("wide", "tp"),
            P("wide"),
            P("wide"),
            P("wide", None),
            P("wide", None, "tp"),
            P("wide", "tp", None),
            P(),
        ),
        check_vma=False,
    )
```

profile of v0, /device:TPU:0, one launch (start us, length us, event | category | flops | bytes accessed | tf_op | source)
XLA Modules:
  0.0 507.1 jit_solution(14593613991823395686)
XLA Ops:
  10.3 1.7 concatenate.15
  14.5 1.9 convolution_convert_fusion.7
  16.4 31.7 %all_to_all.25 = bf16[8,80,768]{2,1,0:T(8,128)(2,1)} all-to-all(bf16[8,80,768]{2,1,0:T(8,128)(2,1)S(1)} %bitcast.79), channel_id=1, replica_groups=mesh['wide'=8,'tp'=4] {'wide'}, dimensions={0} | all-to-all | bytes 1966080 | tf_op jit(solution)/shard_map/all_to_all | solution.py:314
  50.0 35.9 %all-gather.10.cloned.1.call-done = bf16[768,786]{1,0:T(8,128)(2,1)} async-done(((bf16[96,786]{1,0:T(8,128)(2,1)}), bf16[768,786]{1,0:T(8,128)(2,1)}) %all-gather.10.cloned.1.call-update) | async-done | bytes 1207312 | tf_op jit(solution)/shard_map/all_gather | solution.py:292
  89.1 2.5 fusion.77
  92.0 1.3 broadcast_select_fusion
  93.3 3.5 fusion.9
  97.5 2.7 convolution_convert_fusion.4.q_ref.k_ref.v_ref
  100.2 18.0 %attend.1 = (bf16[2048,256]{1,0:T(8,128)(2,1)S(1)}, f32[8,8,256]{2,1,0:T(8,128)S(1)}) custom-call(bf16[2048,768]{1,0:T(8,128)(2,1)S(1)} %convolution_convert_fusion.4.q_ref.k_ref.v_ref, bf16[2048,768]{1,0:T(8,128)(2,1)S(1)} %convolution_convert_fusion.4.q_ref.k_ref.v_ref, bf16[2048,768]{1,0:T(8,128)(2,1)S(1)} %convolution_convert_fusion.4.q_ref.k_ref.v_ref, ...), custom_call_target="tpu_custom_call" | custom-call | tf_op jit(solution)/shard_map/attend/pallas_call | solution.py:210
  118.2 1.7 copy-done.2
  119.9 3.7 convolution_convert_fusion.3
  124.8 36.1 %reduce-scatter.5.cloned.1.call-done = bf16[512,768]{1,0:T(8,128)(2,1)} async-done(((bf16[2048,768]{1,0:T(8,128)(2,1)}), bf16[512,768]{1,0:T(8,128)(2,1)}) %reduce-scatter.5.cloned.1.call-update) | async-done | bytes 786448 | tf_op jit(solution)/shard_map/reduce_scatter | solution.py:67
  160.9 1.7 multiply_reduce_fusion.3
  162.6 1.7 multiply_convert_fusion.3
  165.0 30.4 %all_to_all.26 = bf16[8,80,768]{2,1,0:T(8,128)(2,1)} all-to-all(bf16[8,80,768]{2,1,0:T(8,128)(2,1)S(1)} %bitcast.80), channel_id=1, replica_groups=mesh['wide'=8,'tp'=4] {'wide'}, dimensions={0} | all-to-all | bytes 1966080 | tf_op jit(solution)/shard_map/all_to_all | solution.py:314
  195.4 31.1 %all-gather.14.cloned.1.call-done = bf16[2560,768]{1,0:T(8,128)(2,1)} async-done(((bf16[640,768]{1,0:T(8,128)(2,1)}), bf16[2560,768]{1,0:T(8,128)(2,1)}) %all-gather.14.cloned.1.call-update) | async-done | bytes 3932176 | tf_op jit(solution)/shard_map/all_gather | solution.py:63
  226.5 2.5 copy.112
  229.1 1.9 copy-done.5
  231.0 3.3 fusion.86
  234.3 5.0 convolution_convert_fusion.1
  239.3 2.3 copy.113
  241.7 4.3 copy.114
  246.0 4.5 fusion.81
  250.5 10.6 %fusion.8 = bf16[2,1280,768]{2,1,0:T(8,128)(2,1)S(1)} fusion(f32[2,1280,768]{2,1,0:T(8,128)} %copy-done.54, bf16[2,1280,768]{2,1,0:T(8,128)(2,1)} %bitcast.69, bf16[2,768,768]{2,1,0:T(8,128)(2,1)S(1)} %copy-done, f32[2,1280]{1,0:T(2,128)} %fusion.81), kind=kOutput, calls=%fused_computation.10 | convolution fusion | flops 3061186560 | bytes 18098176 | tf_op jit(solution)/shard_map/ecd,efd->ecf/dot_general | solution.py:361
  261.1 3.5 convolution_convert_fusion
  264.7 2.2 copy.115
  266.9 17.7 %reduce-scatter.7.cloned.1.call-done = bf16[640,768]{1,0:T(8,128)(2,1)} async-done(((bf16[2560,768]{1,0:T(8,128)(2,1)}), bf16[640,768]{1,0:T(8,128)(2,1)}) %reduce-scatter.7.cloned.1.call-update) | async-done | bytes 983056 | tf_op jit(solution)/shard_map/reduce_scatter | solution.py:325
  284.6 5.6 %all-to-all-start.2 = ((bf16[8,80,768]{2,1,0:T(8,128)(2,1)}), bf16[8,80,768]{2,1,0:T(8,128)(2,1)S(1)}, u32[]{:S(2)}, u32[]{:S(2)}) async-start(bf16[8,80,768]{2,1,0:T(8,128)(2,1)} %bitcast.76), calls=%async_computation.4 | async-start | bytes 1966080 | tf_op jit(solution)/shard_map/all_to_all | solution.py:327
  290.3 40.4 %reduce-scatter.9.cloned.1.call-done = bf16[640,768]{1,0:T(8,128)(2,1)} async-done(((bf16[2560,768]{1,0:T(8,128)(2,1)}), bf16[640,768]{1,0:T(8,128)(2,1)}) %reduce-scatter.9.cloned.1.call-update) | async-done | bytes 983056 | tf_op jit(solution)/shard_map/reduce_scatter | solution.py:325
  330.6 5.5 %all-to-all-start.3 = ((bf16[8,80,768]{2,1,0:T(8,128)(2,1)}), bf16[8,80,768]{2,1,0:T(8,128)(2,1)}, u32[]{:S(2)}, u32[]{:S(2)}) async-start(bf16[8,80,768]{2,1,0:T(8,128)(2,1)} %bitcast.77), calls=%async_computation.6 | async-start | bytes 1966080 | tf_op jit(solution)/shard_map/all_to_all | solution.py:327
  337.6 3.6 fusion.27
  342.4 2.5 fusion.54
  344.9 15.8 %all-to-all-done.3 = bf16[8,80,768]{2,1,0:T(8,128)(2,1)} async-done(((bf16[8,80,768]{2,1,0:T(8,128)(2,1)}), bf16[8,80,768]{2,1,0:T(8,128)(2,1)}, u32[]{:S(2)}, u32[]{:S(2)}) %all-to-all-start.3) | async-done | bytes 983072 | tf_op jit(solution)/shard_map/all_to_all | solution.py:327
  360.7 3.8 multiply_reduce_fusion.1
  365.6 1.5 fusion.74
  367.2 8.9 %fusion.87 = f32[2,768,768]{2,1,0:T(8,128)} fusion(bf16[2,1280,768]{2,1,0:T(8,128)(2,1)} %bitcast.64, bf16[2,1280,768]{2,1,0:T(8,128)(2,1)} %copy-done.55), kind=kOutput, calls=%fused_computation.143 | convolution fusion | flops 3019898880 | bytes 12582912 | tf_op jit(solution)/shard_map/ecd,ecf->edf/dot_general | solution.py:388
  376.2 8.7 %fusion.12 = f32[2,768,768]{2,1,0:T(8,128)} fusion(bf16[2,1280,768]{2,1,0:T(8,128)(2,1)S(1)} %bitcast.70, f32[2,1280]{1,0:T(2,128)S(1)} %copy-done.39, f32[2,1280,768]{2,1,0:T(8,128)} %copy-done.54), kind=kOutput, calls=%fused_computation.20 | convolution fusion | flops 3043491840 | bytes 16525312 | tf_op jit(solution)/shard_map/ecf,ecd->efd/dot_general | solution.py:385
  386.3 7.6 %all-gather.16.cloned.1.call-done = bf16[2048,768]{1,0:T(8,128)(2,1)} async-done(((bf16[512,768]{1,0:T(8,128)(2,1)}), bf16[2048,768]{1,0:T(8,128)(2,1)}) %all-gather.16.cloned.1.call-update) | async-done | bytes 3145744 | tf_op jit(solution)/shard_map/all_gather | solution.py:63
  393.9 3.8 fusion.88
  398.7 33.4 %attend_back.1 = (bf16[2048,256]{1,0:T(8,128)(2,1)S(1)}, bf16[2048,256]{1,0:T(8,128)(2,1)S(1)}, bf16[2048,256]{1,0:T(8,128)(2,1)S(1)}, f32[8,2048]{1,0:T(8,128)S(1)}) custom-call(bf16[2048,768]{1,0:T(8,128)(2,1)} %copy-done.2, bf16[2048,768]{1,0:T(8,128)(2,1)} %copy-done.2, bf16[2048,768]{1,0:T(8,128)(2,1)} %copy-done.2, ...), custom_call_target="tpu_custom_call" | custom-call | tf_op jit(solution)/shard_map/attend_back/pallas_call | solution.py:232
  432.3 1.7 copy-done.14
  434.2 4.3 multiply_reduce_fusion
  438.5 4.0 convolution_convert_fusion.2
  445.2 1.6 copy.118
  446.8 5.5 %all-to-all-start.4 = ((bf16[8,96,806]{2,1,0:T(8,128)(2,1)}), bf16[8,96,806]{2,1,0:T(8,128)(2,1)S(1)}, u32[]{:S(2)}, u32[]{:S(2)}) async-start(bf16[8,96,806]{2,1,0:T(8,128)(2,1)} %bitcast.67), calls=%async_computation.8 | async-start | bytes 2752512 | tf_op jit(solution)/shard_map/all_to_all | solution.py:444
  452.4 33.2 %all-to-all-done.4 = bf16[8,96,806]{2,1,0:T(8,128)(2,1)S(1)} async-done(((bf16[8,96,806]{2,1,0:T(8,128)(2,1)}), bf16[8,96,806]{2,1,0:T(8,128)(2,1)S(1)}, u32[]{:S(2)}, u32[]{:S(2)}) %all-to-all-start.4) | async-done | bytes 1238048 | tf_op jit(solution)/shard_map/all_to_all | solution.py:444
  488.0 5.2 %all-gather.1 = f32[4,96,19]{1,2,0:T(8,128)S(1)} all-gather(f32[1,96,19]{1,2,0:T(8,128)S(1)} %copy.119), channel_id=2, replica_groups=mesh['wide'=8,'tp'=4] {'tp'}, dimensions={0}, use_global_device_ids=true | all-gather | bytes 36480 | tf_op jit(solution)/shard_map/all_gather | solution.py:461
  495.5 4.6 fusion.26
  (190 shorter events, 27.8 us)
Async XLA Ops:
  7.2 227.1 %copy-start = (bf16[2,768,768]{2,1,0:T(8,128)(2,1)S(1)}, bf16[2,768,768]{2,1,0:T(8,128)(2,1)}, u32[]{:S(2)}) copy-start(bf16[2,768,768]{2,1,0:T(8,128)(2,1)} %param.24) | copy-start | bytes 7077892
  7.2 40.9 %all-gather.8.cloned.1.call-start = ((), (), s32[]{:S(2)}) async-start(), calls=%async_computation.9 | async-start | bytes 3932160 | tf_op jit(solution)/shard_map/all_gather | solution.py:63
  7.9 78.0 %all-gather.10.cloned.1.call-start = ((), (), s32[]{:S(2)}) async-start(), calls=%async_computation.10 | async-start | bytes 1548288 | tf_op jit(solution)/shard_map/all_gather | solution.py:292
  12.0 107.9 %all-gather.12.cloned.1.call-start = ((), (), s32[]{:S(2)}) async-start(), calls=%async_computation.11 | async-start | bytes 4915200 | tf_op jit(solution)/shard_map/all_gather | solution.py:63
  14.5 149.8 %copy-start.47 = (s32[512]{0:T(512)}, s32[512]{0:T(512)S(1)}, u32[]{:S(2)}) copy-start(s32[512]{0:T(512)S(1)} %convert_add_fusion.2) | copy-start | bytes 6148
  14.5 33.7 %copy-start.49 = (s32[7]{0:T(128)S(1)}, s32[7]{0:T(128)}, u32[]{:S(2)}) copy-start(s32[7]{0:T(128)} %constant.66.clone) | copy-start | bytes 88
  48.1 112.8 %reduce-scatter.5.cloned.1.call-start = ((), (), s32[]{:S(2)}) async-start(), calls=%async_computation.12 | async-start | bytes 3932160 | tf_op jit(solution)/shard_map/reduce_scatter | solution.py:67
  87.1 4.8 copy-start.33
  91.8 5.1 copy-start.22
  92.0 4.9 copy-start.24
  92.0 5.5 %copy-start.13 = (bf16[2048,768]{1,0:T(8,128)(2,1)S(1)}, bf16[2048,768]{1,0:T(8,128)(2,1)}, u32[]{:S(2)}) copy-start(bf16[2048,768]{1,0:T(8,128)(2,1)} %all-gather.8.cloned.1.call-done) | copy-start | bytes 9437188
  123.6 102.9 %all-gather.14.cloned.1.call-start = ((), (), s32[]{:S(2)}) async-start(), calls=%async_computation.13 | async-start | bytes 4915200 | tf_op jit(solution)/shard_map/all_gather | solution.py:63
  164.3 31.1 %copy-start.8 = (bf16[512,768]{1,0:T(8,128)(2,1)}, bf16[512,768]{1,0:T(8,128)(2,1)S(1)}, u32[]{:S(2)}) copy-start(bf16[512,768]{1,0:T(8,128)(2,1)S(1)} %multiply_convert_fusion.3) | copy-start | bytes 2359300
  195.4 89.2 %reduce-scatter.7.cloned.1.call-start = ((), (), s32[]{:S(2)}) async-start(), calls=%async_computation.14 | async-start | bytes 4915200 | tf_op jit(solution)/shard_map/reduce_scatter | solution.py:325
  226.5 4.4 copy-start.52
  234.3 5.0 copy-start.54
  241.6 89.1 %reduce-scatter.9.cloned.1.call-start = ((), (), s32[]{:S(2)}) async-start(), calls=%async_computation.15 | async-start | bytes 4915200 | tf_op jit(solution)/shard_map/reduce_scatter | solution.py:325
  250.5 10.6 %copy-start.53 = (bf16[2,768,768]{2,1,0:T(8,128)(2,1)S(1)}, bf16[2,768,768]{2,1,0:T(8,128)(2,1)}, u32[]{:S(2)}) copy-start(bf16[2,768,768]{2,1,0:T(8,128)(2,1)} %param.23) | copy-start | bytes 7077892
  266.9 69.3 %copy-start.9 = (bf16[512,768]{1,0:T(8,128)(2,1)S(1)}, bf16[512,768]{1,0:T(8,128)(2,1)}, u32[]{:S(2)}) copy-start(bf16[512,768]{1,0:T(8,128)(2,1)} %copy-done.8) | copy-start | bytes 2359300
  284.6 52.9 %copy-start.26 = (s32[512,1]{0,1:T(1,128)S(1)}, s32[512,1]{0,1:T(1,128)}, u32[]{:S(2)}) copy-start(s32[512,1]{0,1:T(1,128)} %param.26) | copy-start | bytes 6148
  284.6 46.0 %all-to-all-start.2 = ((bf16[8,80,768]{2,1,0:T(8,128)(2,1)}), bf16[8,80,768]{2,1,0:T(8,128)(2,1)S(1)}, u32[]{:S(2)}, u32[]{:S(2)}) async-start(bf16[8,80,768]{2,1,0:T(8,128)(2,1)} %bitcast.76), calls=%async_computation.4 | async-start | bytes 1966080 | tf_op jit(solution)/shard_map/all_to_all | solution.py:327
  330.6 7.0 %copy-start.16 = (bf16[8,80,768]{2,1,0:T(8,128)(2,1)}, bf16[8,80,768]{2,1,0:T(8,128)(2,1)S(1)}, u32[]{:S(2)}) copy-start(bf16[8,80,768]{2,1,0:T(8,128)(2,1)S(1)} %all-to-all-done.2) | copy-start | bytes 2949124
  330.6 30.0 %all-to-all-start.3 = ((bf16[8,80,768]{2,1,0:T(8,128)(2,1)}), bf16[8,80,768]{2,1,0:T(8,128)(2,1)}, u32[]{:S(2)}, u32[]{:S(2)}) async-start(bf16[8,80,768]{2,1,0:T(8,128)(2,1)} %bitcast.77), calls=%async_computation.6 | async-start | bytes 1966080 | tf_op jit(solution)/shard_map/all_to_all | solution.py:327
  336.2 57.7 %all-gather.16.cloned.1.call-start = ((), (), s32[]{:S(2)}) async-start(), calls=%async_computation.16 | async-start | bytes 3932160 | tf_op jit(solution)/shard_map/all_gather | solution.py:63
  336.2 5.0 copy-start.40
  337.6 23.1 %copy-start.3 = (bf16[512,768]{1,0:T(8,128)(2,1)S(1)}, bf16[512,768]{1,0:T(8,128)(2,1)}, u32[]{:S(2)}) copy-start(bf16[512,768]{1,0:T(8,128)(2,1)} %param.15) | copy-start | bytes 2359300
  337.6 23.0 %copy-start.7 = (bf16[512,768]{1,0:T(8,128)(2,1)S(1)}, bf16[512,768]{1,0:T(8,128)(2,1)}, u32[]{:S(2)}) copy-start(bf16[512,768]{1,0:T(8,128)(2,1)} %reduce-scatter.5.cloned.1.call-done) | copy-start | bytes 2359300
  360.7 5.0 copy-start.12
  360.7 5.0 copy-start.30
  367.1 9.0 %copy-start.39 = (f32[2,1280]{1,0:T(2,128)S(1)}, f32[2,1280]{1,0:T(2,128)}, u32[]{:S(2)}) copy-start(f32[2,1280]{1,0:T(2,128)} %fusion.81) | copy-start | bytes 30724
  367.1 119.5 %reduce-scatter.11.cloned.1.call-start = ((), (), s32[]{:S(2)}) async-start(), calls=%async_computation.17 | async-start | bytes 3932160 | tf_op jit(solution)/shard_map/reduce_scatter | solution.py:67
  367.2 8.9 %copy-start.11 = (bf16[2,4,8,40,768]{4,3,2,1,0:T(8,128)(2,1)S(1)}, bf16[2,4,8,40,768]{4,3,2,1,0:T(8,128)(2,1)}, u32[]{:S(2)}) copy-start(bf16[2,4,8,40,768]{4,3,2,1,0:T(8,128)(2,1)} %copy.114) | copy-start | bytes 11796484
  376.1 8.7 %copy-start.46 = (f32[768]{0:T(1024)S(1)}, f32[768]{0:T(1024)}, u32[]{:S(2)}) copy-start(f32[768]{0:T(1024)} %get-tuple-element.94) | copy-start | bytes 9220
  376.1 9.3 %copy-start.18 = (f32[512,16]{0,1:T(8,128)S(1)}, f32[512,16]{0,1:T(8,128)}, u32[]{:S(2)}) copy-start(f32[512,16]{0,1:T(8,128)} %copy-done.17) | copy-start | bytes 98308
  376.2 9.3 %copy-start.28 = (f32[512]{0:T(512)S(1)}, f32[512]{0:T(512)}, u32[]{:S(2)}) copy-start(f32[512]{0:T(512)} %copy-done.27) | copy-start | bytes 6148
  376.2 9.3 %copy-start.36 = (f32[512]{0:T(512)S(1)}, f32[512]{0:T(512)}, u32[]{:S(2)}) copy-start(f32[512]{0:T(512)} %copy-done.35) | copy-start | bytes 6148
  386.3 11.4 %copy-start.15 = (bf16[768,192]{1,0:T(8,128)(2,1)S(1)}, bf16[768,192]{1,0:T(8,128)(2,1)}, u32[]{:S(2)}) copy-start(bf16[768,192]{1,0:T(8,128)(2,1)} %get-tuple-element.101) | copy-start | bytes 884740
  438.5 4.7 copy-start.34
  438.5 4.8 copy-start.19
  438.5 4.8 copy-start.32
  445.2 7.1 %copy-start.48 = (f32[512]{0:T(512)S(1)}, f32[512]{0:T(512)}, u32[]{:S(2)}) copy-start(f32[512]{0:T(512)} %get-tuple-element.96) | copy-start | bytes 6148
  446.8 38.7 %all-to-all-start.4 = ((bf16[8,96,806]{2,1,0:T(8,128)(2,1)}), bf16[8,96,806]{2,1,0:T(8,128)(2,1)S(1)}, u32[]{:S(2)}, u32[]{:S(2)}) async-start(bf16[8,96,806]{2,1,0:T(8,128)(2,1)} %bitcast.67), calls=%async_computation.8 | async-start | bytes 2752512 | tf_op jit(solution)/shard_map/all_to_all | solution.py:444
  452.3 42.0 %copy-start.4 = (bf16[512,768]{1,0:T(8,128)(2,1)S(1)}, bf16[512,768]{1,0:T(8,128)(2,1)}, u32[]{:S(2)}) copy-start(bf16[512,768]{1,0:T(8,128)(2,1)} %param.15) | copy-start | bytes 2359300
  486.6 8.9 %copy-start.31 = (f32[512]{0:T(512)S(1)}, f32[512]{0:T(512)}, u32[]{:S(2)}) copy-start(f32[512]{0:T(512)} %copy-done.29) | copy-start | bytes 6148
  486.6 8.9 %copy-start.38 = (f32[512]{0:T(512)S(1)}, f32[512]{0:T(512)}, u32[]{:S(2)}) copy-start(f32[512]{0:T(512)} %copy-done.37) | copy-start | bytes 6148
  486.6 8.9 %copy-start.45 = (f32[512]{0:T(512)S(1)}, f32[512]{0:T(512)}, u32[]{:S(2)}) copy-start(f32[512]{0:T(512)} %get-tuple-element.114) | copy-start | bytes 6148
  487.9 6.5 %copy-start.6 = (f32[512,768]{1,0:T(8,128)}, f32[512,768]{1,0:T(8,128)S(1)}, u32[]{:S(2)}) copy-start(f32[512,768]{1,0:T(8,128)S(1)} %convert_element_type.182) | copy-start | bytes 4718596
  495.5 4.7 copy-start.1
  (21 other events, 49.5 us)
Sparse Core Ops, SparseCore 0:
  9.6 31.2 all-gather.7
  43.6 42.3 all-gather.9
  87.5 31.5 all-gather.11
  123.7 37.1 reduce-scatter.4
  195.5 30.9 all-gather.13
  241.7 42.8 reduce-scatter.6
  287.7 42.8 reduce-scatter.8
  367.2 26.5 all-gather.15
  445.4 37.9 reduce-scatter.10
where the time goes:
time: 516 us; the launch traced here: 507 us
  waiting for transfers between devices  218 us (42%)
  matrix products  81.2 us (16%)
  blocking collectives  67.2 us (13%)
  Pallas kernels  51.4 us (10%)
  local copies, waits for them, and re-layouts  37 us (7%)
  other arithmetic  19.7 us (4%)
  starting transfers between devices  17 us (3%)
  between operations  15.1 us (3%)
    all_to_all x2, blocking collectives, to_wide(): lax.all_to_all(placed, 'wide', split_axis=0, concat_axis=0, tiled=True)  62 us
    reduce_scatter x2, waiting for transfers between devices, from_owners(): summed = lax.psum_scatter(terms, 'tp', scatter_dimension=0, tiled=True)  58 us
    all_gather x4, waiting for transfers between devices, gather_rows(): return lax.all_gather(rows, 'tp', axis=0, tiled=True)  38.7 us
    reduce_scatter x2, waiting for transfers between devices, sum_rows(): lax.psum_scatter(term.astype(jnp.bfloat16), 'tp', scatter_dimension=0, ti...  36.1 us
    all_gather x1, waiting for transfers between devices, per_device(): packed = lax.all_gather(packed, 'wide', axis=0, tiled=True)  35.9 us
    pallas_call x1, Pallas kernels, attend_back(): pl.pallas_call(partial(backward_kernel, heads), grid=(rows // LEN, blocks...  33.4 us
    all_to_all x1, waiting for transfers between devices, per_device(): lax.all_to_all(weight_grads.reshape(wide_size, shard, 4 * head_width + 2...  33.2 us
    pallas_call x1, Pallas kernels, attend(): pl.pallas_call(partial(forward_kernel, heads), grid=(rows // LEN, blocks)...  18 us
  transfers between devices with their start and end apart: 12, of which 8 were waited for; matrix products, arithmetic and copies ran while one was open for 16% of the time, Pallas kernels for 4%

commit v1 on v0

--- a/solution.py
+++ b/solution.py
@@ -276,7 +276,6 @@
     capacity = (5 * tok_rows + 4 * experts - 1) // (4 * experts)
     head_width = query_weight.shape[1]
     local_heads = head_width // HEAD
-    tokens_all = gather_rows(tokens)
     packed = jnp.concatenate(
         [
             query_weight,
@@ -290,6 +289,9 @@
         axis=1,
     )
     packed = lax.all_gather(packed, "wide", axis=0, tiled=True)
+    kept = cotangent * keep.astype(jnp.bfloat16)[:, None]
+    packed, kept, tokens = lax.optimization_barrier((packed, kept, tokens))
+    tokens_all = gather_rows(tokens)
     side = ((0, 0), (0, BLOCK - head_width))
     w_query, w_key, w_value, w_out = (
         jnp.pad(packed[:, i * head_width : (i + 1) * head_width], side) for i in range(4)
@@ -327,7 +329,6 @@
         back = lax.all_to_all(summed, "wide", split_axis=0, concat_axis=0, tiled=True)
         return back.reshape(experts * capacity, width)
 
-    kept = cotangent * keep.astype(jnp.bfloat16)[:, None]
     kept_wide = to_wide(kept)
     onehot_table = bucket_onehot(LEN, BUCKETS)
     table_local = lax.dynamic_slice_in_dim(

time: 516 us -> 519 us (level)
  waiting for transfers between devices: 218 us -> 226 us
    all_gather x1, waiting for transfers between devices: 35.9 us -> 43.1 us  [per_device(): packed = lax.all_gather(packed, 'wide', axis=0, tiled=True)]
    unnamed x120 -> x112, local copies, waits for them, and re-layouts: 11 us -> 9 us
  transfers between devices with their start and end apart: 12 -> 12, of which waited for: 8 -> 9; matrix products, arithmetic and copies ran while one was open for 16% -> 14% of each run, Pallas kernels for 4% -> 4%
where the time goes in v1:
time: 519 us; the launch traced here: 510 us
  waiting for transfers between devices  226 us (44%)
  matrix products  79.3 us (15%)
  blocking collectives  62.4 us (12%)
  Pallas kernels  51.4 us (10%)
  local copies, waits for them, and re-layouts  36.4 us (7%)
  other arithmetic  21.4 us (4%)
  starting transfers between devices  17.7 us (3%)
  between operations  15.1 us (3%)
    reduce_scatter x2, waiting for transfers between devices, from_owners(): summed = lax.psum_scatter(terms, 'tp', scatter_dimension=0, tiled=True)  58.1 us
    all_to_all x2, blocking collectives, to_wide(): lax.all_to_all(placed, 'wide', split_axis=0, concat_axis=0, tiled=True)  57.2 us
    all_gather x1, waiting for transfers between devices, per_device(): packed = lax.all_gather(packed, 'wide', axis=0, tiled=True)  43.1 us
    all_gather x4, waiting for transfers between devices, gather_rows(): return lax.all_gather(rows, 'tp', axis=0, tiled=True)  38.5 us
    reduce_scatter x2, waiting for transfers between devices, sum_rows(): lax.psum_scatter(term.astype(jnp.bfloat16), 'tp', scatter_dimension=0, ti...  37.1 us
    pallas_call x1, Pallas kernels, attend_back(): pl.pallas_call(partial(backward_kernel, heads), grid=(rows // LEN, blocks...  33.4 us
    all_to_all x1, waiting for transfers between devices, per_device(): lax.all_to_all(weight_grads.reshape(wide_size, shard, 4 * head_width + 2...  33.2 us
    pallas_call x1, Pallas kernels, attend(): pl.pallas_call(partial(forward_kernel, heads), grid=(rows // LEN, blocks)...  18 us
  transfers between devices with their start and end apart: 12, of which 9 were waited for; matrix products, arithmetic and copies ran while one was open for 14% of the time, Pallas kernels for 4%

profile of v1, /device:TPU:0, one launch (start us, length us, event | category | flops | bytes accessed | tf_op | source)
XLA Modules:
  0.0 510.0 jit_solution(4478212825168700592)
XLA Ops:
  9.7 1.7 concatenate.15
  13.5 43.1 %all-gather.8.cloned.1.call-done = bf16[768,786]{1,0:T(8,128)(2,1)} async-done(((bf16[96,786]{1,0:T(8,128)(2,1)}), bf16[768,786]{1,0:T(8,128)(2,1)}) %all-gather.8.cloned.1.call-update) | async-done | bytes 1207312 | tf_op jit(solution)/shard_map/all_gather | solution.py:291
  57.7 27.3 %all_to_all.25 = bf16[8,80,768]{2,1,0:T(8,128)(2,1)} all-to-all(bf16[8,80,768]{2,1,0:T(8,128)(2,1)S(1)} %bitcast.78), channel_id=1, replica_groups=mesh['wide'=8,'tp'=4] {'wide'}, dimensions={0} | all-to-all | bytes 1966080 | tf_op jit(solution)/shard_map/all_to_all | solution.py:316
  87.2 2.0 slice.75
  89.3 2.5 copy.107
  95.0 3.3 fusion.9
  98.4 2.7 convolution_convert_fusion.4.q_ref.k_ref.v_ref
  101.1 18.0 %attend.1 = (bf16[2048,256]{1,0:T(8,128)(2,1)S(1)}, f32[8,8,256]{2,1,0:T(8,128)S(1)}) custom-call(bf16[2048,768]{1,0:T(8,128)(2,1)S(1)} %convolution_convert_fusion.4.q_ref.k_ref.v_ref, bf16[2048,768]{1,0:T(8,128)(2,1)S(1)} %convolution_convert_fusion.4.q_ref.k_ref.v_ref, bf16[2048,768]{1,0:T(8,128)(2,1)S(1)} %convolution_convert_fusion.4.q_ref.k_ref.v_ref, ...), custom_call_target="tpu_custom_call" | custom-call | tf_op jit(solution)/shard_map/attend/pallas_call | solution.py:210
  119.2 1.7 copy-done.2
  120.9 3.7 convolution_convert_fusion.3
  125.8 37.1 %reduce-scatter.5.cloned.1.call-done = bf16[512,768]{1,0:T(8,128)(2,1)} async-done(((bf16[2048,768]{1,0:T(8,128)(2,1)}), bf16[512,768]{1,0:T(8,128)(2,1)}) %reduce-scatter.5.cloned.1.call-update) | async-done | bytes 786448 | tf_op jit(solution)/shard_map/reduce_scatter | solution.py:67
  162.9 1.7 multiply_reduce_fusion.3
  164.6 1.7 multiply_convert_fusion.3
  166.3 1.4 convolution_convert_fusion.6
  167.7 29.9 %all_to_all.26 = bf16[8,80,768]{2,1,0:T(8,128)(2,1)} all-to-all(bf16[8,80,768]{2,1,0:T(8,128)(2,1)S(1)} %bitcast.79), channel_id=1, replica_groups=mesh['wide'=8,'tp'=4] {'wide'}, dimensions={0} | all-to-all | bytes 1966080 | tf_op jit(solution)/shard_map/all_to_all | solution.py:316
  198.2 30.6 %all-gather.14.cloned.1.call-done = bf16[2560,768]{1,0:T(8,128)(2,1)} async-done(((bf16[640,768]{1,0:T(8,128)(2,1)}), bf16[2560,768]{1,0:T(8,128)(2,1)}) %all-gather.14.cloned.1.call-update) | async-done | bytes 3932176 | tf_op jit(solution)/shard_map/all_gather | solution.py:63
  228.8 2.5 copy.112
  231.3 1.9 copy-done.5
  233.2 3.3 fusion.85
  236.5 5.0 convolution_convert_fusion.1
  241.5 2.3 copy.113
  243.9 4.3 copy.114
  248.2 4.5 fusion.80
  252.8 10.6 %fusion.8 = bf16[2,1280,768]{2,1,0:T(8,128)(2,1)S(1)} fusion(f32[2,1280,768]{2,1,0:T(8,128)} %copy-done.52, bf16[2,1280,768]{2,1,0:T(8,128)(2,1)} %bitcast.69, bf16[2,768,768]{2,1,0:T(8,128)(2,1)S(1)} %copy-done, f32[2,1280]{1,0:T(2,128)} %fusion.80), kind=kOutput, calls=%fused_computation.10 | convolution fusion | flops 3061186560 | bytes 18098176 | tf_op jit(solution)/shard_map/ecd,efd->ecf/dot_general | solution.py:362
  263.3 3.5 convolution_convert_fusion
  266.9 2.2 copy.115
  269.1 17.7 %reduce-scatter.7.cloned.1.call-done = bf16[640,768]{1,0:T(8,128)(2,1)} async-done(((bf16[2560,768]{1,0:T(8,128)(2,1)}), bf16[640,768]{1,0:T(8,128)(2,1)}) %reduce-scatter.7.cloned.1.call-update) | async-done | bytes 983056 | tf_op jit(solution)/shard_map/reduce_scatter | solution.py:327
  286.8 5.6 %all-to-all-start.2 = ((bf16[8,80,768]{2,1,0:T(8,128)(2,1)}), bf16[8,80,768]{2,1,0:T(8,128)(2,1)}, u32[]{:S(2)}, u32[]{:S(2)}) async-start(bf16[8,80,768]{2,1,0:T(8,128)(2,1)} %bitcast.76), calls=%async_computation.4 | async-start | bytes 1966080 | tf_op jit(solution)/shard_map/all_to_all | solution.py:329
  292.5 40.4 %reduce-scatter.9.cloned.1.call-done = bf16[640,768]{1,0:T(8,128)(2,1)} async-done(((bf16[2560,768]{1,0:T(8,128)(2,1)}), bf16[640,768]{1,0:T(8,128)(2,1)}) %reduce-scatter.9.cloned.1.call-update) | async-done | bytes 983056 | tf_op jit(solution)/shard_map/reduce_scatter | solution.py:327
  332.9 5.5 %all-to-all-start.3 = ((bf16[8,80,768]{2,1,0:T(8,128)(2,1)}), bf16[8,80,768]{2,1,0:T(8,128)(2,1)}, u32[]{:S(2)}, u32[]{:S(2)}) async-start(bf16[8,80,768]{2,1,0:T(8,128)(2,1)} %bitcast.77), calls=%async_computation.6 | async-start | bytes 1966080 | tf_op jit(solution)/shard_map/all_to_all | solution.py:329
  339.8 3.4 fusion.27
  344.3 2.3 fusion.55
  346.6 16.3 %all-to-all-done.3 = bf16[8,80,768]{2,1,0:T(8,128)(2,1)} async-done(((bf16[8,80,768]{2,1,0:T(8,128)(2,1)}), bf16[8,80,768]{2,1,0:T(8,128)(2,1)}, u32[]{:S(2)}, u32[]{:S(2)}) %all-to-all-start.3) | async-done | bytes 983072 | tf_op jit(solution)/shard_map/all_to_all | solution.py:329
  362.9 3.7 multiply_reduce_fusion.1
  367.8 1.5 fusion.73
  369.4 8.9 %fusion.86 = f32[2,768,768]{2,1,0:T(8,128)} fusion(bf16[2,1280,768]{2,1,0:T(8,128)(2,1)} %bitcast.64, bf16[2,1280,768]{2,1,0:T(8,128)(2,1)} %copy-done.53), kind=kOutput, calls=%fused_computation.143 | convolution fusion | flops 3019898880 | bytes 12582912 | tf_op jit(solution)/shard_map/ecd,ecf->edf/dot_general | solution.py:389
  378.4 8.7 %fusion.12 = f32[2,768,768]{2,1,0:T(8,128)} fusion(bf16[2,1280,768]{2,1,0:T(8,128)(2,1)S(1)} %bitcast.70, f32[2,1280]{1,0:T(2,128)S(1)} %copy-done.37, f32[2,1280,768]{2,1,0:T(8,128)} %copy-done.52), kind=kOutput, calls=%fused_computation.20 | convolution fusion | flops 3043491840 | bytes 16525312 | tf_op jit(solution)/shard_map/ecf,ecd->efd/dot_general | solution.py:386
  388.5 7.6 %all-gather.16.cloned.1.call-done = bf16[2048,768]{1,0:T(8,128)(2,1)} async-done(((bf16[512,768]{1,0:T(8,128)(2,1)}), bf16[2048,768]{1,0:T(8,128)(2,1)}) %all-gather.16.cloned.1.call-update) | async-done | bytes 3145744 | tf_op jit(solution)/shard_map/all_gather | solution.py:63
  396.0 3.8 fusion.87
  400.8 33.4 %attend_back.1 = (bf16[2048,256]{1,0:T(8,128)(2,1)S(1)}, bf16[2048,256]{1,0:T(8,128)(2,1)S(1)}, bf16[2048,256]{1,0:T(8,128)(2,1)S(1)}, f32[8,2048]{1,0:T(8,128)S(1)}) custom-call(bf16[2048,768]{1,0:T(8,128)(2,1)} %copy-done.2, bf16[2048,768]{1,0:T(8,128)(2,1)} %copy-done.2, bf16[2048,768]{1,0:T(8,128)(2,1)} %copy-done.2, ...), custom_call_target="tpu_custom_call" | custom-call | tf_op jit(solution)/shard_map/attend_back/pallas_call | solution.py:232
  434.5 1.7 copy-done.15
  436.4 4.3 multiply_reduce_fusion
  440.7 3.9 convolution_convert_fusion.2
  448.1 1.6 copy.118
  449.7 5.5 %all-to-all-start.4 = ((bf16[8,96,806]{2,1,0:T(8,128)(2,1)}), bf16[8,96,806]{2,1,0:T(8,128)(2,1)S(1)}, u32[]{:S(2)}, u32[]{:S(2)}) async-start(bf16[8,96,806]{2,1,0:T(8,128)(2,1)} %bitcast.67), calls=%async_computation.8 | async-start | bytes 2752512 | tf_op jit(solution)/shard_map/all_to_all | solution.py:445
  455.2 33.2 %all-to-all-done.4 = bf16[8,96,806]{2,1,0:T(8,128)(2,1)S(1)} async-done(((bf16[8,96,806]{2,1,0:T(8,128)(2,1)}), bf16[8,96,806]{2,1,0:T(8,128)(2,1)S(1)}, u32[]{:S(2)}, u32[]{:S(2)}) %all-to-all-start.4) | async-done | bytes 1238048 | tf_op jit(solution)/shard_map/all_to_all | solution.py:445
  490.8 5.2 %all-gather.1 = f32[4,96,19]{1,2,0:T(8,128)S(1)} all-gather(f32[1,96,19]{1,2,0:T(8,128)S(1)} %copy.119), channel_id=2, replica_groups=mesh['wide'=8,'tp'=4] {'tp'}, dimensions={0}, use_global_device_ids=true | all-gather | bytes 36480 | tf_op jit(solution)/shard_map/all_gather | solution.py:462
  498.3 4.6 fusion.26
  (183 shorter events, 27.7 us)
Async XLA Ops:
  7.2 229.3 %copy-start = (bf16[2,768,768]{2,1,0:T(8,128)(2,1)S(1)}, bf16[2,768,768]{2,1,0:T(8,128)(2,1)}, u32[]{:S(2)}) copy-start(bf16[2,768,768]{2,1,0:T(8,128)(2,1)} %param.24) | copy-start | bytes 7077892
  7.2 49.5 %copy-start.26 = (s32[512,1]{0,1:T(1,128)S(1)}, s32[512,1]{0,1:T(1,128)}, u32[]{:S(2)}) copy-start(s32[512,1]{0,1:T(1,128)} %param.26) | copy-start | bytes 6148
  7.2 49.4 %all-gather.8.cloned.1.call-start = ((), (), s32[]{:S(2)}) async-start(), calls=%async_computation.9 | async-start | bytes 1548288 | tf_op jit(solution)/shard_map/all_gather | solution.py:291
  11.4 73.8 %all-gather.10.cloned.1.call-start = ((), (), s32[]{:S(2)}) async-start(), calls=%async_computation.10 | async-start | bytes 3932160 | tf_op jit(solution)/shard_map/all_gather | solution.py:63
  56.6 64.3 %all-gather.12.cloned.1.call-start = ((), (), s32[]{:S(2)}) async-start(), calls=%async_computation.11 | async-start | bytes 4915200 | tf_op jit(solution)/shard_map/all_gather | solution.py:63
  57.0 28.0 %copy-start.45 = (s32[512]{0:T(512)}, s32[512]{0:T(512)S(1)}, u32[]{:S(2)}) copy-start(s32[512]{0:T(512)S(1)} %convert_add_fusion.2) | copy-start | bytes 6148
  57.0 28.4 %copy-start.47 = (s32[7]{0:T(128)S(1)}, s32[7]{0:T(128)}, u32[]{:S(2)}) copy-start(s32[7]{0:T(128)} %constant.66.clone) | copy-start | bytes 88
  85.3 7.2 %copy-start.48 = (pred[256]{0:T(512)(128)(4,1)S(1)}, pred[256]{0:T(512)(128)(4,1)}, u32[]{:S(2)}) copy-start(pred[256]{0:T(512)(128)(4,1)} %constant.17.clone.1) | copy-start | bytes 772
  85.3 77.6 %reduce-scatter.5.cloned.1.call-start = ((), (), s32[]{:S(2)}) async-start(), calls=%async_computation.12 | async-start | bytes 3932160 | tf_op jit(solution)/shard_map/reduce_scatter | solution.py:67
  93.6 4.8 copy-start.20
  93.6 4.8 copy-start.14
  124.6 104.2 %all-gather.14.cloned.1.call-start = ((), (), s32[]{:S(2)}) async-start(), calls=%async_computation.13 | async-start | bytes 4915200 | tf_op jit(solution)/shard_map/all_gather | solution.py:63
  166.3 31.3 %copy-start.9 = (bf16[512,768]{1,0:T(8,128)(2,1)}, bf16[512,768]{1,0:T(8,128)(2,1)S(1)}, u32[]{:S(2)}) copy-start(bf16[512,768]{1,0:T(8,128)(2,1)S(1)} %multiply_convert_fusion.3) | copy-start | bytes 2359300
  197.6 89.2 %reduce-scatter.7.cloned.1.call-start = ((), (), s32[]{:S(2)}) async-start(), calls=%async_computation.14 | async-start | bytes 4915200 | tf_op jit(solution)/shard_map/reduce_scatter | solution.py:327
  228.8 4.4 copy-start.50
  236.5 5.0 copy-start.52
  243.8 89.1 %reduce-scatter.9.cloned.1.call-start = ((), (), s32[]{:S(2)}) async-start(), calls=%async_computation.15 | async-start | bytes 4915200 | tf_op jit(solution)/shard_map/reduce_scatter | solution.py:327
  252.7 10.6 %copy-start.51 = (bf16[2,768,768]{2,1,0:T(8,128)(2,1)S(1)}, bf16[2,768,768]{2,1,0:T(8,128)(2,1)}, u32[]{:S(2)}) copy-start(bf16[2,768,768]{2,1,0:T(8,128)(2,1)} %param.23) | copy-start | bytes 7077892
  269.1 69.5 %copy-start.10 = (bf16[512,768]{1,0:T(8,128)(2,1)S(1)}, bf16[512,768]{1,0:T(8,128)(2,1)}, u32[]{:S(2)}) copy-start(bf16[512,768]{1,0:T(8,128)(2,1)} %copy-done.9) | copy-start | bytes 2359300
  286.8 53.0 %copy-start.8 = (bf16[512,768]{1,0:T(8,128)(2,1)S(1)}, bf16[512,768]{1,0:T(8,128)(2,1)}, u32[]{:S(2)}) copy-start(bf16[512,768]{1,0:T(8,128)(2,1)} %param.28) | copy-start | bytes 2359300
  286.8 46.0 %all-to-all-start.2 = ((bf16[8,80,768]{2,1,0:T(8,128)(2,1)}), bf16[8,80,768]{2,1,0:T(8,128)(2,1)}, u32[]{:S(2)}, u32[]{:S(2)}) async-start(bf16[8,80,768]{2,1,0:T(8,128)(2,1)} %bitcast.76), calls=%async_computation.4 | async-start | bytes 1966080 | tf_op jit(solution)/shard_map/all_to_all | solution.py:329
  332.9 30.0 %all-to-all-start.3 = ((bf16[8,80,768]{2,1,0:T(8,128)(2,1)}), bf16[8,80,768]{2,1,0:T(8,128)(2,1)}, u32[]{:S(2)}, u32[]{:S(2)}) async-start(bf16[8,80,768]{2,1,0:T(8,128)(2,1)} %bitcast.77), calls=%async_computation.6 | async-start | bytes 1966080 | tf_op jit(solution)/shard_map/all_to_all | solution.py:329
  338.4 57.6 %all-gather.16.cloned.1.call-start = ((), (), s32[]{:S(2)}) async-start(), calls=%async_computation.16 | async-start | bytes 3932160 | tf_op jit(solution)/shard_map/all_gather | solution.py:63
  338.6 4.6 copy-start.38
  339.7 4.1 copy-start.17
  339.7 4.0 copy-start.27
  339.8 23.1 %copy-start.3 = (bf16[512,768]{1,0:T(8,128)(2,1)S(1)}, bf16[512,768]{1,0:T(8,128)(2,1)}, u32[]{:S(2)}) copy-start(bf16[512,768]{1,0:T(8,128)(2,1)} %param.15) | copy-start | bytes 2359300
  339.8 23.1 %copy-start.7 = (bf16[512,768]{1,0:T(8,128)(2,1)S(1)}, bf16[512,768]{1,0:T(8,128)(2,1)}, u32[]{:S(2)}) copy-start(bf16[512,768]{1,0:T(8,128)(2,1)} %reduce-scatter.5.cloned.1.call-done) | copy-start | bytes 2359300
  362.9 4.9 copy-start.30
  369.3 9.0 %copy-start.37 = (f32[2,1280]{1,0:T(2,128)S(1)}, f32[2,1280]{1,0:T(2,128)}, u32[]{:S(2)}) copy-start(f32[2,1280]{1,0:T(2,128)} %fusion.80) | copy-start | bytes 30724
  369.3 120.2 %reduce-scatter.11.cloned.1.call-start = ((), (), s32[]{:S(2)}) async-start(), calls=%async_computation.17 | async-start | bytes 3932160 | tf_op jit(solution)/shard_map/reduce_scatter | solution.py:67
  369.4 8.9 %copy-start.13 = (bf16[2,4,8,40,768]{4,3,2,1,0:T(8,128)(2,1)S(1)}, bf16[2,4,8,40,768]{4,3,2,1,0:T(8,128)(2,1)}, u32[]{:S(2)}) copy-start(bf16[2,4,8,40,768]{4,3,2,1,0:T(8,128)(2,1)} %copy.114) | copy-start | bytes 11796484
  378.3 8.7 %copy-start.44 = (f32[768]{0:T(1024)S(1)}, f32[768]{0:T(1024)}, u32[]{:S(2)}) copy-start(f32[768]{0:T(1024)} %get-tuple-element.100) | copy-start | bytes 9220
  378.3 9.3 %copy-start.11 = (bf16[512,768]{1,0:T(8,128)(2,1)S(1)}, bf16[512,768]{1,0:T(8,128)(2,1)}, u32[]{:S(2)}) copy-start(bf16[512,768]{1,0:T(8,128)(2,1)} %copy-done.9) | copy-start | bytes 2359300
  378.3 9.3 %copy-start.18 = (f32[512,16]{0,1:T(8,128)S(1)}, f32[512,16]{0,1:T(8,128)}, u32[]{:S(2)}) copy-start(f32[512,16]{0,1:T(8,128)} %copy-done.17) | copy-start | bytes 98308
  378.3 9.3 %copy-start.28 = (f32[512]{0:T(512)S(1)}, f32[512]{0:T(512)}, u32[]{:S(2)}) copy-start(f32[512]{0:T(512)} %copy-done.27) | copy-start | bytes 6148
  378.3 9.3 %copy-start.34 = (f32[512]{0:T(512)S(1)}, f32[512]{0:T(512)}, u32[]{:S(2)}) copy-start(f32[512]{0:T(512)} %copy-done.33) | copy-start | bytes 6148
  388.5 11.4 %copy-start.16 = (bf16[768,192]{1,0:T(8,128)(2,1)S(1)}, bf16[768,192]{1,0:T(8,128)(2,1)}, u32[]{:S(2)}) copy-start(bf16[768,192]{1,0:T(8,128)(2,1)} %slice.75) | copy-start | bytes 884740
  440.7 5.4 %copy-start.19 = (f32[768,16]{0,1:T(8,128)S(1)}, f32[768,16]{0,1:T(8,128)}, u32[]{:S(2)}) copy-start(f32[768,16]{0,1:T(8,128)} %fusion.70) | copy-start | bytes 147460
  440.7 5.5 %copy-start.32 = (f32[768,1]{0,1:T(1,128)S(1)}, f32[768,1]{0,1:T(1,128)}, u32[]{:S(2)}) copy-start(f32[768,1]{0,1:T(1,128)} %broadcast_in_dim.15) | copy-start | bytes 9220
  448.1 7.1 %copy-start.46 = (f32[512]{0:T(512)S(1)}, f32[512]{0:T(512)}, u32[]{:S(2)}) copy-start(f32[512]{0:T(512)} %get-tuple-element.102) | copy-start | bytes 6148
  449.7 38.7 %all-to-all-start.4 = ((bf16[8,96,806]{2,1,0:T(8,128)(2,1)}), bf16[8,96,806]{2,1,0:T(8,128)(2,1)S(1)}, u32[]{:S(2)}, u32[]{:S(2)}) async-start(bf16[8,96,806]{2,1,0:T(8,128)(2,1)} %bitcast.67), calls=%async_computation.8 | async-start | bytes 2752512 | tf_op jit(solution)/shard_map/all_to_all | solution.py:445
  455.2 42.0 %copy-start.4 = (bf16[512,768]{1,0:T(8,128)(2,1)S(1)}, bf16[512,768]{1,0:T(8,128)(2,1)}, u32[]{:S(2)}) copy-start(bf16[512,768]{1,0:T(8,128)(2,1)} %param.15) | copy-start | bytes 2359300
  489.5 8.9 %copy-start.31 = (f32[512]{0:T(512)S(1)}, f32[512]{0:T(512)}, u32[]{:S(2)}) copy-start(f32[512]{0:T(512)} %copy-done.29) | copy-start | bytes 6148
  489.5 8.9 %copy-start.36 = (f32[512]{0:T(512)S(1)}, f32[512]{0:T(512)}, u32[]{:S(2)}) copy-start(f32[512]{0:T(512)} %copy-done.35) | copy-start | bytes 6148
  489.5 8.9 %copy-start.43 = (f32[512]{0:T(512)S(1)}, f32[512]{0:T(512)}, u32[]{:S(2)}) copy-start(f32[512]{0:T(512)} %get-tuple-element.119) | copy-start | bytes 6148
  490.7 6.5 %copy-start.6 = (f32[512,768]{1,0:T(8,128)}, f32[512,768]{1,0:T(8,128)S(1)}, u32[]{:S(2)}) copy-start(f32[512,768]{1,0:T(8,128)S(1)} %convert_element_type.182) | copy-start | bytes 4718596
  498.3 4.7 copy-start.1
  (19 other events, 43.8 us)
Sparse Core Ops, SparseCore 0:
  11.6 44.9 all-gather.7
  58.2 27.0 all-gather.9
  86.8 32.9 all-gather.11
  124.7 38.1 reduce-scatter.4
  197.8 30.9 all-gather.13
  243.9 42.8 reduce-scatter.6
  289.9 42.8 reduce-scatter.8
  369.4 26.5 all-gather.15
  448.2 37.9 reduce-scatter.10
